TPU v7x, 32 devices: a whole 2x2x4 slice. The times are simulated.
32 devices in a mesh: pole: 2 (over y), row: 4 (over z), col: 4 (over x, core).
Axes of the slice: x: 2, y: 2, z: 4, core: 2. Of those that a mesh axis runs over, the one named last changes fastest.
Arguments:
- inverse_top: bfloat16 [2048, 1024], P(('pole', 'row'), 'col'), parts along dimension 0
- factor_first: bfloat16 [8, 256, 1024], P(('pole', 'col'), 'row'), parts along dimension 0, may hold values from -0.75 to 0.75
- factor_second: bfloat16 [8, 256, 1024], P(('pole', 'col'), 'row'), parts along dimension 0, may hold values from -0.75 to 0.75
- parent_factor: bfloat16 [2048, 256], P(('pole', 'col')), parts along dimension 0, may hold values from -0.75 to 0.75
- diag_first_inv: float32 [2048, 256], P(('pole', 'col')), parts along dimension 0, may hold values from -6 to 6
- diag_second_inv: float32 [2048, 256], P(('pole', 'col')), parts along dimension 0, may hold values from -6 to 6
- pattern_first: int32 [4, 4], replicated, may hold values 0 or 1
- pattern_second: int32 [4, 4], replicated, may hold values 0 or 1
- parent: int32 [4, 1], replicated, may hold values from 0 to 3
Outputs:
- x_first: bfloat16 [2048, 1024], P(('pole', 'row'), 'col'), parts along dimension 0
- diag_first: bfloat16 [2048, 256], P(('pole', 'col')), parts along dimension 0
- x_second: bfloat16 [2048, 1024], P(('pole', 'row'), 'col'), parts along dimension 0
- cross_second: bfloat16 [2048, 256], P(('pole', 'col')), parts along dimension 0
- diag_second: float32 [2048, 256], P(('pole', 'col')), parts along dimension 0
There are 2 independent parts, one for each index of `pole`. A program takes and returns all parts, laid end to end along the dimension named above; an argument that names none is the same for every part. Nothing has to cross between parts.
Inputs may be any that keep to these rules, and one draw needn't show every extreme that they name: `pattern_first`: 1 where the block row lies in the supernode's structure. `pattern_second`: 1 where the block row may lie in the supernode's structure. Every level-one supernode is the parent of some level-two supernode.
All inputs are finite; a program needn't handle non-finite values.
Results may differ from a plain program's by a relative error of at most 0.0053.
Values may be sent and summed in bfloat16 or wider, within the bound.
A program may use at most 64 MiB of HBM per device.

v0:
```python
import jax
import jax.numpy as jnp
from jax import lax
from jax.sharding import PartitionSpec as P


def broadcast(value, axis, source):
    kept = jnp.where(lax.axis_index(axis) == source, value, 0).astype(value.dtype)
    return lax.psum(kept, axis)


def spread_factor(masked):
    return lax.all_gather(masked, "row", axis=1, tiled=True)


def column_sums(parts):
    return lax.psum(parts, "row")


def on_device(
    inverse_top,
    factor_first,
    factor_second,
    parent_factor,
    diag_first_inv,
    diag_second_inv,
    pattern_first,
    pattern_second,
    parent,
):
    f32 = jnp.float32
    bf16 = jnp.bfloat16
    col_index = lax.axis_index("col")
    row_index = lax.axis_index("row")
    width = inverse_top.shape[0]
    blocks_col = factor_first.shape[0]
    local_first = diag_first_inv.shape[0] // width
    local_second = diag_second_inv.shape[0] // width
    total_first = pattern_first.shape[1]
    onehot = (parent == jnp.arange(total_first, dtype=jnp.int32)[None, :]).astype(jnp.int32)
    mask_second = pattern_second * jnp.sum(pattern_first[:, None, :] * onehot[None, :, :], axis=2)

    def column_mask(pattern):
        rows_here = lax.dynamic_slice_in_dim(pattern, col_index * blocks_col, blocks_col, 0)
        return jnp.repeat(rows_here, width, axis=1).astype(bf16)[:, None, :]

    def row_mask(pattern, count):
        piece = lax.dynamic_slice(pattern, (row_index, col_index * count), (1, count))
        return jnp.repeat(piece, width, axis=1).astype(f32)

    def owner_block(gathered, count):
        root = row_index // blocks_col
        pick = jnp.clip(row_index - col_index * blocks_col, 0, blocks_col - 1)
        own_all = broadcast(
            lax.dynamic_index_in_dim(gathered, pick, 0, keepdims=False), "col", root
        )
        return lax.dynamic_slice_in_dim(own_all, col_index * count * width, count * width, 1)

    def level_products(gathered, count):
        flat = gathered.reshape(-1, gathered.shape[2])
        summed = lax.psum_scatter(
            lax.dot_general(
                flat, inverse_top, (((0,), (1,)), ((), ())), preferred_element_type=f32
            ),
            "col",
            scatter_dimension=0,
            tiled=True,
        )
        own = owner_block(gathered, count)
        return (summed.T, own)

    masked_first = factor_first * column_mask(pattern_first)
    masked_second = factor_second * column_mask(mask_second)
    gathered_first = spread_factor(masked_first)
    z_first, own_first = level_products(gathered_first, local_first)
    x_first = (-(row_mask(pattern_first, local_first) * z_first)).astype(bf16)
    shape_first = (width, local_first, width)
    partial_first = jnp.einsum(
        "wsa,wsb->sab",
        own_first.reshape(shape_first),
        x_first.reshape(shape_first),
        preferred_element_type=f32,
    )
    summed_first = column_sums(partial_first)
    diag_first = (
        (diag_first_inv.reshape(local_first, width, width) - summed_first)
        .astype(bf16)
        .reshape(-1, width)
    )
    x_all, diag_all = (
        lax.all_gather(x_first, "col", axis=1, tiled=True),
        lax.all_gather(diag_first, "col", axis=0, tiled=True),
    )
    parent_here = lax.dynamic_slice_in_dim(parent, col_index * local_second, local_second, 0)
    select = (parent_here == jnp.arange(total_first, dtype=jnp.int32)[None, :]).astype(bf16)
    x_parent = jnp.einsum(
        "wkb,sk->wsb", x_all.reshape(width, total_first, width), select, preferred_element_type=f32
    ).astype(bf16)
    a_parent = jnp.einsum(
        "kab,sk->sab",
        diag_all.reshape(total_first, width, width),
        select,
        preferred_element_type=f32,
    ).astype(bf16)
    gathered_second = spread_factor(masked_second)
    z_second, own_second = level_products(gathered_second, local_second)
    below = parent_factor.reshape(local_second, width, width)
    z_second = z_second + jnp.einsum(
        "wsa,sab->wsb", x_parent, below, preferred_element_type=f32
    ).reshape(width, -1)
    x_second = (-(row_mask(mask_second, local_second) * z_second)).astype(bf16)
    shape_second = (width, local_second, width)
    own_blocks = own_second.reshape(shape_second)
    cross_part, inner_part = column_sums(
        (
            jnp.einsum("wsa,wsb->sab", x_parent, own_blocks, preferred_element_type=f32),
            jnp.einsum(
                "wsa,wsb->sab",
                own_blocks,
                x_second.reshape(shape_second),
                preferred_element_type=f32,
            ),
        )
    )
    cross = (
        -(cross_part + jnp.einsum("sak,skb->sab", a_parent, below, preferred_element_type=f32))
    ).astype(bf16)
    diag_second = (
        diag_second_inv.reshape(local_second, width, width)
        - inner_part
        - jnp.einsum("sab,sac->sbc", below, cross, preferred_element_type=f32)
    )
    return (x_first, diag_first, x_second, cross.reshape(-1, width), diag_second.reshape(-1, width))


def solution(mesh):
    in_specs = (
        P(("pole", "row"), "col"),
        P(("pole", "col"), "row", None),
        P(("pole", "col"), "row", None),
        P(("pole", "col"), None),
        P(("pole", "col"), None),
        P(("pole", "col"), None),
        P(),
        P(),
        P(),
    )
    out_specs = (
        P(("pole", "row"), "col"),
        P(("pole", "col"), None),
        P(("pole", "row"), "col"),
        P(("pole", "col"), None),
        P(("pole", "col"), None),
    )
    return jax.shard_map(
        on_device, mesh=mesh, in_specs=in_specs, out_specs=out_specs, check_vma=False
    )
```

profile of v0, /device:TPU:0, one launch (start us, length us, event | category | flops | bytes accessed | tf_op | source)
XLA Modules:
  0.0 189.8 jit_solution(17909458652711675709)
XLA Ops:
  7.2 0.0 copy-start
  7.2 0.0 reduce-scatter.3.cloned.1.call-start
  7.2 0.7 copy-done.12
  7.9 0.1 fusion.20
  8.0 0.6 copy-done.10
  8.6 0.1 multiply_reduce_fusion
  8.7 0.5 copy-done.11
  9.3 0.1 broadcast_bitcast_fusion.1
  9.4 0.9 broadcast_multiply_fusion.1
  10.3 17.4 %all_gather.12 = bf16[1,256,1024]{2,1,0:T(8,128)(2,1)S(1)} all-gather(bf16[1,64,1024]{2,1,0:T(8,128)(2,1)S(1)} %broadcast_multiply_fusion.1), channel_id=1, replica_groups=mesh['pole'=2,'row'=4,'col'=4] {'row'}, dimensions={1}, use_global_device_ids=true | all-gather | bytes 655360 | tf_op jit(solution)/shard_map/all_gather | solution.py:13
  27.7 1.3 fusion.11
  29.0 0.0 reduce-scatter.3.cloned.1.call-update
  29.0 0.0 all-reduce.7.cloned.1.call-start
  29.1 0.1 broadcast_bitcast_fusion
  29.2 0.7 copy-done.9
  29.9 16.3 %all_gather.13 = bf16[1,256,1024]{2,1,0:T(8,128)(2,1)S(1)} all-gather(bf16[1,64,1024]{2,1,0:T(8,128)(2,1)S(1)} %broadcast_multiply_fusion), channel_id=1, replica_groups=mesh['pole'=2,'row'=4,'col'=4] {'row'}, dimensions={1}, use_global_device_ids=true | all-gather | bytes 655360 | tf_op jit(solution)/shard_map/all_gather | solution.py:13
  46.2 0.8 bitcast_select_fusion.1
  47.0 0.8 bitcast_select_fusion
  47.9 0.0 all-reduce.7.cloned.1.call-update
  47.9 0.0 reduce-scatter.5.cloned.1.call-start
  48.0 1.3 fusion.9
  49.3 0.0 reduce-scatter.5.cloned.1.call-update
  49.3 0.0 all-reduce.5.cloned.1.call-start
  49.4 0.6 constant_dynamic-slice_fusion
  50.0 0.6 dynamic_slice.24
  50.5 0.6 dynamic_slice.27
  52.4 3.4 %reduce-scatter.3.cloned.1.call-done = f32[256,256]{1,0:T(8,128)} async-done(((f32[1024,256]{1,0:T(8,128)}), f32[256,256]{1,0:T(8,128)}) %reduce-scatter.3.cloned.1.call-update) | async-done | bytes 262160 | tf_op jit(solution)/shard_map/reduce_scatter | solution.py:61
  55.8 1.0 fusion.19
  56.8 6.8 %all_gather.14 = bf16[256,1024]{0,1:T(8,128)(2,1)S(1)} all-gather(bf16[256,256]{0,1:T(8,128)(2,1)S(1)} %fusion.19), channel_id=1, replica_groups=mesh['pole'=2,'row'=4,'col'=4] {'col'}, dimensions={1}, use_global_device_ids=true | all-gather | bytes 655360 | tf_op jit(solution)/shard_map/all_gather | solution.py:91
  63.6 0.3 copy.22
  63.9 1.0 fusion.28
  64.9 29.7 %all-reduce.7.cloned.1.call-done = (bf16[256,1024]{1,0:T(8,128)(2,1)}, bf16[256,1024]{1,0:T(8,128)(2,1)}) async-done(((bf16[256,1024]{1,0:T(8,128)(2,1)}, bf16[256,1024]{1,0:T(8,128)(2,1)}), (bf16[256,1024]{1,0:T(8,128)(2,1)}, bf16[256,1024]{1,0:T(8,128)(2,1)})) %all-reduce.7.cloned.1.call-update) | async-done | bytes 1048592 | tf_op jit(solution)/shard_map/psum | solution.py:9
  94.6 1.9 convolution_bitcast_fusion.3
  96.5 26.0 %reduce-scatter.5.cloned.1.call-done = f32[256,256]{1,0:T(8,128)} async-done(((f32[1024,256]{1,0:T(8,128)}), f32[256,256]{1,0:T(8,128)}) %reduce-scatter.5.cloned.1.call-update) | async-done | bytes 262160 | tf_op jit(solution)/shard_map/reduce_scatter | solution.py:61
  122.5 1.2 fusion.7
  123.7 1.9 convolution_bitcast_fusion.1
  125.6 1.8 convolution_bitcast_fusion.4
  127.4 0.0 all-reduce.5.cloned.1.call-update
  127.4 0.8 copy.21
  128.2 0.8 copy.20
  129.0 43.0 %all-reduce.5.cloned.1.call-done = (f32[1,256,256]{2,1,0:T(8,128)}, f32[1,256,256]{2,1,0:T(8,128)}, f32[1,256,256]{2,1,0:T(8,128)}) async-done(((f32[1,256,256]{2,1,0:T(8,128)}, f32[1,256,256]{2,1,0:T(8,128)}, f32[1,256,256]{2,1,0:T(8,128)}), (f32[1,256,256]{2,1,0:T(8,128)}, f32[1,256,256]{2,1,0:T(8,128)}, f32[1,256,256]{2,1,0:T(8,128)})) %all-reduce.5.cloned.1.call-update) | async-done | bytes 786448 | tf_op jit(solution)/shard_map/psum | solution.py:17
  172.0 1.0 fusion.15
  173.0 7.2 %all-gather = bf16[1,1024,256]{2,1,0:T(8,128)(2,1)S(1)} all-gather(bf16[1,256,256]{2,1,0:T(8,128)(2,1)S(1)} %fusion.15), channel_id=2, replica_groups=mesh['pole'=2,'row'=4,'col'=4] {'col'}, dimensions={1}, use_global_device_ids=true | all-gather | bytes 655360 | tf_op jit(solution)/shard_map/all_gather | solution.py:92
  180.1 1.2 fusion.13
  181.3 0.2 fusion.8
  181.5 0.7 copy-done.7
  182.2 0.1 copy-done.8
  182.3 0.9 fusion.5
  (24 shorter events, 0.1 us)
Async XLA Ops:
  7.2 20.5 %copy-start = (bf16[256,256]{1,0:T(8,128)(2,1)S(1)}, bf16[256,256]{1,0:T(8,128)(2,1)}, u32[]{:S(2)}) copy-start(bf16[256,256]{1,0:T(8,128)(2,1)} %param.9) | copy-start | bytes 393220
  7.2 48.6 %reduce-scatter.3.cloned.1.call-start = ((), (), s32[]{:S(2)}) async-start(), calls=%async_computation.2 | async-start | bytes 1310720 | tf_op jit(solution)/shard_map/reduce_scatter | solution.py:61
  7.2 0.7 copy-start.12
  7.9 0.7 copy-start.10
  8.6 0.7 copy-start.11
  29.0 0.9 copy-start.9
  29.0 65.6 %all-reduce.7.cloned.1.call-start = ((), (), s32[]{:S(2)}) async-start(), calls=%async_computation.5 | async-start | bytes 2097152 | tf_op jit(solution)/shard_map/psum | solution.py:9
  47.9 74.6 %reduce-scatter.5.cloned.1.call-start = ((), (), s32[]{:S(2)}) async-start(), calls=%async_computation.3 | async-start | bytes 1310720 | tf_op jit(solution)/shard_map/reduce_scatter | solution.py:61
  49.3 122.6 %all-reduce.5.cloned.1.call-start = ((), (), s32[]{:S(2)}) async-start(), calls=%async_computation.4 | async-start | bytes 1572864 | tf_op jit(solution)/shard_map/psum | solution.py:17
  94.6 27.9 %copy-start.1 = (bf16[256,256]{1,0:T(8,128)(2,1)S(1)}, bf16[256,256]{1,0:T(8,128)(2,1)}, u32[]{:S(2)}) copy-start(bf16[256,256]{1,0:T(8,128)(2,1)} %param.12) | copy-start | bytes 393220
  123.7 1.9 %copy-start.2 = (f32[256,256]{1,0:T(8,128)S(1)}, f32[256,256]{1,0:T(8,128)}, u32[]{:S(2)}) copy-start(f32[256,256]{1,0:T(8,128)} %reduce-scatter.3.cloned.1.call-done) | copy-start | bytes 786436
  127.4 44.5 %copy-start.5 = (f32[256,256]{1,0:T(8,128)S(1)}, f32[256,256]{1,0:T(8,128)}, u32[]{:S(2)}) copy-start(f32[256,256]{1,0:T(8,128)} %param.13) | copy-start | bytes 786436
  172.9 7.2 %copy-start.3 = (bf16[1,256,256]{2,1,0:T(8,128)(2,1)}, bf16[1,256,256]{2,1,0:T(8,128)(2,1)S(1)}, u32[]{:S(2)}) copy-start(bf16[1,256,256]{2,1,0:T(8,128)(2,1)S(1)} %fusion.15) | copy-start | bytes 393220
  180.1 1.2 copy-start.6
  181.3 1.0 copy-start.7
  181.3 1.0 copy-start.8
  181.5 1.7 copy-start.4
Sparse Core Ops, SparseCore 0:
  29.1 26.6 reduce-scatter.2
  58.4 36.1 all-reduce.6
  97.2 25.2 reduce-scatter.4
  127.5 44.3 all-reduce.4
where the time goes:
time: 190 us
  waiting for transfers between devices  102 us (54%)
  blocking collectives  47.6 us (25%)
  between operations  15.2 us (8%)
  matrix products  12.8 us (7%)
  local copies, waits for them, and re-layouts  7.15 us (4%)
  other arithmetic  4.78 us (3%)
    psum x1, waiting for transfers between devices, column_sums(): return lax.psum(parts, 'row')  43 us
    all_gather x2, blocking collectives, spread_factor(): return lax.all_gather(masked, 'row', axis=1, tiled=True)  33.6 us
    psum x1, waiting for transfers between devices, broadcast(): return lax.psum(kept, axis)  29.7 us
    reduce_scatter x2, waiting for transfers between devices, level_products(): lax.psum_scatter(lax.dot_general(flat, inverse_top, (((0,), (1,)), ((), (...  29.4 us
    all_gather x1, blocking collectives, on_device(): lax.all_gather(diag_first, 'col', axis=0, tiled=True)  7.16 us
    all_gather x1, blocking collectives, on_device(): lax.all_gather(x_first, 'col', axis=1, tiled=True)  6.76 us
    unnamed x32, local copies, waits for them, and re-layouts  5.1 us
  transfers between devices with their start and end apart: 4, of which 4 were waited for; matrix products, arithmetic and copies ran while one was open for 6% of the time, Pallas kernels for 0%

commit v1 on v0

--- a/solution.py
+++ b/solution.py
@@ -1,6 +1,10 @@
+import functools
+
 import jax
 import jax.numpy as jnp
 from jax import lax
+from jax.experimental import pallas as pl
+from jax.experimental.pallas import tpu as pltpu
 from jax.sharding import PartitionSpec as P
 
 
@@ -17,7 +21,7 @@
     return lax.psum(parts, "row")
 
 
-def on_device(
+def on_device_large(
     inverse_top,
     factor_first,
     factor_second,
@@ -133,6 +137,347 @@
     return (x_first, diag_first, x_second, cross.reshape(-1, width), diag_second.reshape(-1, width))
 
 
+MESH = pl.DeviceIdType.MESH
+VMEM_BUDGET = 48 * 1024 * 1024
+UP, DOWN, ACROSS, SIB, SIB_FAR = range(5)
+INV, ONE, TWO, DIAG = range(4)
+
+
+def fused_kernel(
+    rows,
+    cols,
+    inv_ref,
+    one_ref,
+    two_ref,
+    below_ref,
+    dinv_one_ref,
+    dinv_two_ref,
+    pat_one,
+    pat_two,
+    parent,
+    x_one_ref,
+    diag_one_ref,
+    x_two_ref,
+    cross_ref,
+    diag_two_ref,
+    inv_all,
+    one_all,
+    two_all,
+    diag_all,
+    masked,
+    x_one_all,
+    x_two_all,
+    send_sem,
+    recv_sem,
+    local_sem,
+):
+    f32, bf16 = jnp.float32, jnp.bfloat16
+    width = inv_ref.shape[0]
+    slab = one_ref.shape[0]
+    y = lax.axis_index("pole")
+    z = lax.axis_index("row")
+    c = lax.axis_index("col")
+    sib = c + 1 - 2 * (c % 2)
+    far = (c + 2) % cols
+    far_sib = (sib + 2) % cols
+    devices = {
+        UP: (y, z + 1, c),
+        DOWN: (y, z - 1, c),
+        ACROSS: (y, z, far),
+        SIB: (y, z, sib),
+        SIB_FAR: (y, z, sib),
+    }
+
+    def span(start, size):
+        return pl.ds(pl.multiple_of(start, size), size)
+
+    def columns(lane):
+        if lane in (UP, DOWN):
+            return slice(None)
+        if lane == ACROSS:
+            return span((far // 2) * 2 * width, 2 * width)
+        return span(sib * width, width)
+
+    def arrived(lane):
+        if lane in (UP, DOWN):
+            return slice(None)
+        if lane == ACROSS:
+            return span((c // 2) * 2 * width, 2 * width)
+        return span(c * width, width)
+
+    def place(unit, zs, cs, part):
+        if unit == INV:
+            return inv_all.at[cs, span(zs * width, width), :]
+        if unit == ONE:
+            return one_all.at[cs, zs]
+        if unit == TWO:
+            return two_all.at[cs, zs, :, part]
+        return diag_all.at[cs]
+
+    def origin(unit, part):
+        if unit == INV:
+            return inv_ref
+        if unit == ONE:
+            return one_ref
+        if unit == TWO:
+            return two_ref.at[:, part]
+        return diag_all.at[c]
+
+    def when(conditions, act):
+        if conditions:
+            both = conditions[0]
+            for condition in conditions[1:]:
+                both = jnp.logical_and(both, condition)
+            pl.when(both)(act)
+        else:
+            act()
+
+    sent = []
+
+    def send(unit, zs, cs, lane, own=False, conditions=()):
+        def descriptor():
+            part = columns(lane)
+            return pltpu.make_async_remote_copy(
+                src_ref=origin(unit, part) if own else place(unit, zs, cs, part),
+                dst_ref=place(unit, zs, cs, part),
+                send_sem=send_sem.at[unit, zs, lane],
+                recv_sem=recv_sem.at[unit, zs, cs],
+                device_id=devices[lane],
+                device_id_type=MESH,
+            )
+
+        when(list(conditions), lambda: descriptor().start())
+        sent.append((list(conditions), descriptor))
+
+    def receive(unit, zs, cs, lane, conditions=()):
+        def act():
+            part = arrived(lane)
+            pltpu.make_async_remote_copy(
+                src_ref=place(unit, zs, cs, part),
+                dst_ref=place(unit, zs, cs, part),
+                send_sem=send_sem.at[unit, zs, lane],
+                recv_sem=recv_sem.at[unit, zs, cs],
+                device_id=devices[SIB],
+                device_id_type=MESH,
+            ).wait_recv()
+
+        when(list(conditions), act)
+
+    can_up, can_down = z + 1 < rows, z >= 1
+    diag_all[c] = dinv_one_ref[...].astype(bf16)
+
+    barrier = pltpu.get_barrier_semaphore()
+    for lane, conditions in ((UP, [can_up]), (DOWN, [can_down]), (ACROSS, []), (SIB, [])):
+        when(
+            conditions,
+            lambda lane=lane: pl.semaphore_signal(
+                barrier, inc=1, device_id=devices[lane], device_id_type=MESH
+            ),
+        )
+    pl.semaphore_wait(barrier, 2 + can_up.astype(jnp.int32) + can_down.astype(jnp.int32))
+
+    for unit in (INV, ONE, TWO):
+        send(unit, z, c, UP, True, [can_up])
+        send(unit, z, c, DOWN, True, [can_down])
+        send(unit, z, c, ACROSS, True)
+        send(unit, z, c, SIB, True)
+    local = []
+    for unit in (INV, ONE, TWO):
+        local.append(
+            pltpu.make_async_copy(
+                origin(unit, slice(None)), place(unit, z, c, slice(None)), local_sem.at[unit]
+            )
+        )
+        local[-1].start()
+    send(DIAG, 0, c, ACROSS, True)
+    send(DIAG, 0, c, SIB, True)
+
+    def at_distance(step):
+        if step == 0:
+            return [(z, [], None, [])]
+        return [
+            (z - step, [z - step >= 0], UP, [can_up]),
+            (z + step, [z + step < rows], DOWN, [can_down]),
+        ]
+
+    def pass_across(step):
+        for unit in (INV, ONE, TWO):
+            for zs, exists, _, _ in at_distance(step):
+                receive(unit, zs, far, ACROSS, exists)
+                send(unit, zs, far, SIB_FAR, False, exists)
+
+    for step in range(1, rows):
+        for unit in (INV, ONE, TWO):
+            for zs, exists, lane, further in at_distance(step):
+                receive(unit, zs, c, lane, exists)
+                if step < rows - 1:
+                    send(unit, zs, c, lane, False, exists + further)
+                send(unit, zs, c, ACROSS, False, exists)
+                send(unit, zs, c, SIB, False, exists)
+        pass_across(step - 1)
+        if step == 1:
+            receive(DIAG, 0, far, ACROSS)
+            send(DIAG, 0, far, SIB_FAR)
+    pass_across(rows - 1)
+    for unit in (INV, ONE, TWO):
+        for zs in range(rows):
+            receive(unit, zs, sib, SIB)
+            receive(unit, zs, far_sib, SIB_FAR)
+    receive(DIAG, 0, sib, SIB)
+    receive(DIAG, 0, far_sib, SIB_FAR)
+    for copy in local:
+        copy.wait()
+
+    chosen = [(parent[c, 0] == k).astype(jnp.int32).astype(f32) for k in range(cols)]
+
+    def mask_one(b):
+        return pat_one[b, c].astype(f32)
+
+    def mask_parent(b):
+        return sum(chosen[k] * pat_one[b, k].astype(f32) for k in range(cols))
+
+    def mask_two(b):
+        return pat_two[b, c].astype(f32) * mask_parent(b)
+
+    def gather_columns(slot, source, mask):
+        for b in range(cols):
+            block = source[b, :, :, span(c * width, width)].reshape(width, width)
+            masked[slot, b] = (block.astype(f32) * mask(b)).astype(bf16)
+
+    def gather_parent():
+        for b in range(cols):
+            total = None
+            for k in range(cols):
+                block = one_all[b, :, :, k * width : (k + 1) * width].reshape(width, width)
+                term = block.astype(f32) * (chosen[k] * pat_one[b, k].astype(f32))
+                total = term if total is None else total + term
+            masked[1, b] = total.astype(bf16)
+
+    def dot(a, b, ca=1, cb=0):
+        return lax.dot_general(a, b, (((ca,), (cb,)), ((), ())), preferred_element_type=f32)
+
+    def times_inverse(slot, r):
+        total = None
+        for b in range(cols):
+            term = dot(inv_all[b, r * width : (r + 1) * width, :], masked[slot, b])
+            total = term if total is None else total + term
+        return total
+
+    gather_columns(0, one_all, mask_one)
+    gather_parent()
+    gather_columns(2, two_all, mask_two)
+    below = below_ref[...]
+
+    inner = jnp.zeros((width, width), f32)
+    inner_parent = jnp.zeros((width, width), f32)
+    for r in range(rows):
+        x_own = (-(mask_one(r) * times_inverse(0, r))).astype(bf16)
+        x_one_all[r] = x_own
+        inner += dot(masked[0, r], x_own, 0, 0)
+        x_par = (-(mask_parent(r) * times_inverse(1, r))).astype(bf16)
+        x_two_all[r] = x_par
+        inner_parent += dot(masked[1, r], x_par, 0, 0)
+    x_one_ref[...] = x_one_all[z]
+    diag_one_ref[...] = (dinv_one_ref[...] - inner).astype(bf16)
+    dinv_parent = sum(chosen[k] * diag_all[k].astype(f32) for k in range(cols))
+    diag_parent = (dinv_parent - inner_parent).astype(bf16)
+
+    cross_part = dot(diag_parent, below)
+    inner_two = jnp.zeros((width, width), f32)
+    for r in range(rows):
+        x_par = x_two_all[r]
+        cross_part += dot(x_par, masked[2, r], 0, 0)
+        z_two = times_inverse(2, r) + dot(x_par, below)
+        x_two = (-(mask_two(r) * z_two)).astype(bf16)
+        x_two_all[r] = x_two
+        inner_two += dot(masked[2, r], x_two, 0, 0)
+    x_two_ref[...] = x_two_all[z]
+    cross = (-cross_part).astype(bf16)
+    cross_ref[...] = cross
+    diag_two_ref[...] = dinv_two_ref[...] - inner_two - dot(below, cross, 0, 0)
+
+    for conditions, descriptor in sent:
+        when(conditions, lambda descriptor=descriptor: descriptor().wait_send())
+
+
+def on_device_small(
+    rows,
+    cols,
+    inverse_top,
+    factor_first,
+    factor_second,
+    parent_factor,
+    diag_first_inv,
+    diag_second_inv,
+    pattern_first,
+    pattern_second,
+    parent,
+):
+    bf16 = jnp.bfloat16
+    width = inverse_top.shape[0]
+    slab, wide = factor_first.shape[1:]
+    square = (width, width)
+    vmem = pl.BlockSpec(memory_space=pltpu.VMEM)
+    smem = pl.BlockSpec(memory_space=pltpu.SMEM)
+    shape = jax.ShapeDtypeStruct
+    return pl.pallas_call(
+        functools.partial(fused_kernel, rows, cols),
+        out_shape=(
+            shape(square, bf16),
+            shape(square, bf16),
+            shape(square, bf16),
+            shape(square, bf16),
+            shape(square, jnp.float32),
+        ),
+        in_specs=[vmem] * 6 + [smem] * 3,
+        out_specs=(vmem,) * 5,
+        scratch_shapes=[
+            pltpu.VMEM((cols, rows * width, width), bf16),
+            pltpu.VMEM((cols, rows, slab, wide), bf16),
+            pltpu.VMEM((cols, rows, slab, wide), bf16),
+            pltpu.VMEM((cols,) + square, bf16),
+            pltpu.VMEM((3, cols) + square, bf16),
+            pltpu.VMEM((rows,) + square, bf16),
+            pltpu.VMEM((rows,) + square, bf16),
+            pltpu.SemaphoreType.DMA((4, rows, 5)),
+            pltpu.SemaphoreType.DMA((4, rows, cols)),
+            pltpu.SemaphoreType.DMA((3,)),
+        ],
+        compiler_params=pltpu.CompilerParams(
+            collective_id=0, has_side_effects=True, vmem_limit_bytes=VMEM_BUDGET
+        ),
+    )(
+        inverse_top,
+        factor_first.reshape(slab, wide),
+        factor_second.reshape(slab, wide),
+        parent_factor,
+        diag_first_inv,
+        diag_second_inv,
+        pattern_first,
+        pattern_second,
+        parent,
+    )
+
+
+def on_device(rows, cols, *args):
+    inverse_top, factor_first, factor_second, parent_factor = args[:4]
+    width, depth = inverse_top.shape
+    one_each = (
+        cols == 4
+        and depth == width
+        and factor_first.shape[0] == 1
+        and factor_second.shape == factor_first.shape
+        and factor_first.shape[1] % 16 == 0
+        and factor_first.shape[2] == cols * width
+        and parent_factor.shape[0] == width
+        and rows == cols
+    )
+    gathered = 2 * rows * cols * (inverse_top.size + factor_first.size + factor_second.size)
+    if one_each and gathered <= VMEM_BUDGET // 2:
+        return on_device_small(rows, cols, *args)
+    return on_device_large(*args)
+
+
 def solution(mesh):
     in_specs = (
         P(("pole", "row"), "col"),
@@ -153,5 +498,5 @@
         P(("pole", "col"), None),
     )
     return jax.shard_map(
-        on_device, mesh=mesh, in_specs=in_specs, out_specs=out_specs, check_vma=False
-    )
+        functools.partial(on_device, mesh.shape["row"], mesh.shape["col"]), mesh=mesh, in_specs=in_specs, out_specs=out_specs, check_vma=False
+    )

time: 190 us -> 54 us (0.28)
  waiting for transfers between devices: 102 us -> 0 us
  blocking collectives: 47.6 us -> 0 us
  Pallas kernels: 0 us -> 42.8 us
  between operations: 15.2 us -> 0.67 us
  matrix products: 12.8 us -> 0 us
  other arithmetic: 4.78 us -> 0 us
  local copies, waits for them, and re-layouts: 7.15 us -> 9.57 us
    psum x2 -> x0, waiting for transfers between devices: 72.7 us -> none  [the longest x1 43 us: column_sums(): return lax.psum(parts, 'row')]
    all_gather x4 -> x0, blocking collectives: 47.6 us -> none  [the longest x2 33.6 us: spread_factor(): return lax.all_gather(masked, 'row', axis=1, tiled=True)]
    pallas_call x0 -> x1, Pallas kernels: none -> 42.8 us  [on_device_small(): pl.pallas_call(functools.partial(fused_kernel, rows, cols), out_shape=(sh...]
    reduce_scatter x2 -> x0, waiting for transfers between devices: 29.4 us -> none  [level_products(): lax.psum_scatter(lax.dot_general(flat, inverse_top, (((0,), (1,)), ((), (...]
    dot_general x10 -> x0, matrix products: 12.8 us -> none  [the longest x2 2.68 us: level_products(): lax.dot_general(flat, inverse_top, (((0,), (1,)), ((), ())), preferred_el...]
    unnamed x32 -> x24, local copies, waits for them, and re-layouts: 5.1 us -> 9.57 us
    convert_element_type x4 -> x0, other arithmetic: 2.03 us -> none  [the longest x1 0.98 us: on_device(): diag_first = (diag_first_inv.reshape(local_first, width, width) - summed_...]
  transfers between devices with their start and end apart: 4 -> 0, of which waited for: 4 -> 0; matrix products, arithmetic and copies ran while one was open for 6% -> 0% of each run, Pallas kernels for 0% -> 0%
where the time goes in v1:
time: 54 us; the launch traced here: 53 us
  Pallas kernels  42.8 us (79%)
  local copies, waits for them, and re-layouts  9.57 us (18%)
  between operations  0.67 us (1%)
    pallas_call x1, Pallas kernels, on_device_small(): pl.pallas_call(functools.partial(fused_kernel, rows, cols), out_shape=(sh...  42.8 us
    unnamed x24, local copies, waits for them, and re-layouts  9.57 us

profile of v1, /device:TPU:0, one launch (start us, length us, event | category | flops | bytes accessed | tf_op | source)
XLA Modules:
  0.0 53.0 jit_solution(3113197171573665349)
XLA Ops:
  0.6 0.0 copy-start.8
  0.6 0.0 copy-start.6
  0.7 0.0 copy-start.7
  0.7 0.6 %copy-done.8 = s32[4,1]{0,1:T(1,128)S(1)} copy-done((s32[4,1]{0,1:T(1,128)S(1)}, s32[4,1]{0,1:T(1,128)}, u32[]{:S(2)}) %copy-start.8) | copy-done | bytes 40
  1.3 0.1 copy.14.parent
  1.4 0.0 copy-done.6
  1.4 0.0 copy-done.7
  1.4 0.0 copy-start
  1.4 0.9 %copy-done = f32[256,256]{1,0:T(8,128)S(1)} copy-done((f32[256,256]{1,0:T(8,128)S(1)}, f32[256,256]{1,0:T(8,128)}, u32[]{:S(2)}) %copy-start) | copy-done | bytes 262168
  2.3 0.0 copy-start.1
  2.3 0.9 %copy-done.1 = f32[256,256]{1,0:T(8,128)S(1)} copy-done((f32[256,256]{1,0:T(8,128)S(1)}, f32[256,256]{1,0:T(8,128)}, u32[]{:S(2)}) %copy-start.1) | copy-done | bytes 262168
  3.3 0.0 copy-start.2
  3.3 0.9 %copy-done.2 = bf16[256,256]{1,0:T(8,128)(2,1)S(1)} copy-done((bf16[256,256]{1,0:T(8,128)(2,1)S(1)}, bf16[256,256]{1,0:T(8,128)(2,1)}, u32[]{:S(2)}) %copy-start.2) | copy-done | bytes 131096
  4.2 0.0 copy-start.3
  4.2 0.9 %copy-done.3 = bf16[1,64,1024]{2,1,0:T(8,128)(2,1)S(1)} copy-done((bf16[1,64,1024]{2,1,0:T(8,128)(2,1)S(1)}, bf16[1,64,1024]{2,1,0:T(8,128)(2,1)}, u32[]{:S(2)}) %copy-start.3) | copy-done | bytes 131096
  5.1 0.0 copy-start.4
  5.1 0.9 %copy-done.4 = bf16[1,64,1024]{2,1,0:T(8,128)(2,1)S(1)} copy-done((bf16[1,64,1024]{2,1,0:T(8,128)(2,1)S(1)}, bf16[1,64,1024]{2,1,0:T(8,128)(2,1)}, u32[]{:S(2)}) %copy-start.4) | copy-done | bytes 131096
  6.0 0.0 copy-start.5
  6.0 0.9 %copy-done.5 = bf16[256,256]{1,0:T(8,128)(2,1)S(1)} copy-done((bf16[256,256]{1,0:T(8,128)(2,1)S(1)}, bf16[256,256]{1,0:T(8,128)(2,1)}, u32[]{:S(2)}) %copy-start.5) | copy-done | bytes 131096
  6.9 42.8 %shard_map.128 = (bf16[256,256]{1,0:T(8,128)(2,1)S(1)}, bf16[256,256]{1,0:T(8,128)(2,1)S(1)}, bf16[256,256]{1,0:T(8,128)(2,1)S(1)}, bf16[256,256]{1,0:T(8,128)(2,1)S(1)}, f32[256,256]{1,0:T(8,128)S(1)}) custom-call(bf16[256,256]{1,0:T(8,128)(2,1)S(1)} %copy-done.2, bf16[64,1024]{1,0:T(8,128)(2,1)S(1)} %bitcast.2, bf16[64,1024]{1,0:T(8,128)(2,1)S(1)} %bitcast.3, ...), custom_call_target="tpu_custom_call" | custom-call | tf_op jit(solution)/shard_map/pallas_call | solution.py:423
  49.7 0.7 %copy.20 = bf16[256,256]{1,0:T(8,128)(2,1)} copy(bf16[256,256]{1,0:T(8,128)(2,1)S(1)} %get-tuple-element.10) | data formatting | bytes 262144
  50.3 0.7 %copy.21 = bf16[256,256]{1,0:T(8,128)(2,1)} copy(bf16[256,256]{1,0:T(8,128)(2,1)S(1)} %get-tuple-element.11) | data formatting | bytes 262144
  51.0 0.7 %copy.22 = bf16[256,256]{1,0:T(8,128)(2,1)} copy(bf16[256,256]{1,0:T(8,128)(2,1)S(1)} %get-tuple-element.12) | data formatting | bytes 262144
  51.7 0.7 %copy.23 = bf16[256,256]{1,0:T(8,128)(2,1)} copy(bf16[256,256]{1,0:T(8,128)(2,1)S(1)} %get-tuple-element.13) | data formatting | bytes 262144
  52.3 0.7 %copy.24 = f32[256,256]{1,0:T(8,128)} copy(f32[256,256]{1,0:T(8,128)S(1)} %get-tuple-element.14) | data formatting | bytes 524288
Async XLA Ops:
  0.6 0.7 %copy-start.8 = (s32[4,1]{0,1:T(1,128)S(1)}, s32[4,1]{0,1:T(1,128)}, u32[]{:S(2)}) copy-start(s32[4,1]{0,1:T(1,128)} %param.17) | copy-start | bytes 52
  0.6 0.7 %copy-start.6 = (s32[4,4]{1,0:T(4,128)S(1)}, s32[4,4]{1,0:T(4,128)}, u32[]{:S(2)}) copy-start(s32[4,4]{1,0:T(4,128)} %pat_one.1) | copy-start | bytes 196
  0.7 0.7 %copy-start.7 = (s32[4,4]{1,0:T(4,128)S(1)}, s32[4,4]{1,0:T(4,128)}, u32[]{:S(2)}) copy-start(s32[4,4]{1,0:T(4,128)} %pat_two.1) | copy-start | bytes 196
  1.4 1.0 %copy-start = (f32[256,256]{1,0:T(8,128)S(1)}, f32[256,256]{1,0:T(8,128)}, u32[]{:S(2)}) copy-start(f32[256,256]{1,0:T(8,128)} %dinv_one_ref.1) | copy-start | bytes 786436
  2.3 0.9 %copy-start.1 = (f32[256,256]{1,0:T(8,128)S(1)}, f32[256,256]{1,0:T(8,128)}, u32[]{:S(2)}) copy-start(f32[256,256]{1,0:T(8,128)} %dinv_two_ref.1) | copy-start | bytes 786436
  3.3 0.9 %copy-start.2 = (bf16[256,256]{1,0:T(8,128)(2,1)S(1)}, bf16[256,256]{1,0:T(8,128)(2,1)}, u32[]{:S(2)}) copy-start(bf16[256,256]{1,0:T(8,128)(2,1)} %inv_ref.1) | copy-start | bytes 393220
  4.2 0.9 %copy-start.3 = (bf16[1,64,1024]{2,1,0:T(8,128)(2,1)S(1)}, bf16[1,64,1024]{2,1,0:T(8,128)(2,1)}, u32[]{:S(2)}) copy-start(bf16[1,64,1024]{2,1,0:T(8,128)(2,1)} %param.10) | copy-start | bytes 393220
  5.1 0.9 %copy-start.4 = (bf16[1,64,1024]{2,1,0:T(8,128)(2,1)S(1)}, bf16[1,64,1024]{2,1,0:T(8,128)(2,1)}, u32[]{:S(2)}) copy-start(bf16[1,64,1024]{2,1,0:T(8,128)(2,1)} %param.11) | copy-start | bytes 393220
  6.0 0.9 %copy-start.5 = (bf16[256,256]{1,0:T(8,128)(2,1)S(1)}, bf16[256,256]{1,0:T(8,128)(2,1)}, u32[]{:S(2)}) copy-start(bf16[256,256]{1,0:T(8,128)(2,1)} %below_ref.1) | copy-start | bytes 393220

commit v2 on v1

--- a/solution.py
+++ b/solution.py
@@ -163,6 +163,9 @@
     inv_all,
     one_all,
     two_all,
+    below_own,
+    dinv_one,
+    dinv_two,
     diag_all,
     masked,
     x_one_all,
@@ -214,15 +217,6 @@
             return two_all.at[cs, zs, :, part]
         return diag_all.at[cs]
 
-    def origin(unit, part):
-        if unit == INV:
-            return inv_ref
-        if unit == ONE:
-            return one_ref
-        if unit == TWO:
-            return two_ref.at[:, part]
-        return diag_all.at[c]
-
     def when(conditions, act):
         if conditions:
             both = conditions[0]
@@ -234,11 +228,11 @@
 
     sent = []
 
-    def send(unit, zs, cs, lane, own=False, conditions=()):
+    def send(unit, zs, cs, lane, conditions=()):
         def descriptor():
             part = columns(lane)
             return pltpu.make_async_remote_copy(
-                src_ref=origin(unit, part) if own else place(unit, zs, cs, part),
+                src_ref=place(unit, zs, cs, part),
                 dst_ref=place(unit, zs, cs, part),
                 send_sem=send_sem.at[unit, zs, lane],
                 recv_sem=recv_sem.at[unit, zs, cs],
@@ -264,7 +258,22 @@
         when(list(conditions), act)
 
     can_up, can_down = z + 1 < rows, z >= 1
-    diag_all[c] = dinv_one_ref[...].astype(bf16)
+    everything = slice(None)
+    local = [
+        pltpu.make_async_copy(source, target, local_sem.at[slot])
+        for slot, (source, target) in enumerate(
+            (
+                (inv_ref, place(INV, z, c, everything)),
+                (one_ref, place(ONE, z, c, everything)),
+                (two_ref, place(TWO, z, c, everything)),
+                (below_ref, below_own),
+                (dinv_one_ref, dinv_one),
+                (dinv_two_ref, dinv_two),
+            )
+        )
+    ]
+    for copy in local:
+        copy.start()
 
     barrier = pltpu.get_barrier_semaphore()
     for lane, conditions in ((UP, [can_up]), (DOWN, [can_down]), (ACROSS, []), (SIB, [])):
@@ -276,22 +285,6 @@
         )
     pl.semaphore_wait(barrier, 2 + can_up.astype(jnp.int32) + can_down.astype(jnp.int32))
 
-    for unit in (INV, ONE, TWO):
-        send(unit, z, c, UP, True, [can_up])
-        send(unit, z, c, DOWN, True, [can_down])
-        send(unit, z, c, ACROSS, True)
-        send(unit, z, c, SIB, True)
-    local = []
-    for unit in (INV, ONE, TWO):
-        local.append(
-            pltpu.make_async_copy(
-                origin(unit, slice(None)), place(unit, z, c, slice(None)), local_sem.at[unit]
-            )
-        )
-        local[-1].start()
-    send(DIAG, 0, c, ACROSS, True)
-    send(DIAG, 0, c, SIB, True)
-
     def at_distance(step):
         if step == 0:
             return [(z, [], None, [])]
@@ -300,32 +293,47 @@
             (z + step, [z + step < rows], DOWN, [can_down]),
         ]
 
-    def pass_across(step):
-        for unit in (INV, ONE, TWO):
-            for zs, exists, _, _ in at_distance(step):
-                receive(unit, zs, far, ACROSS, exists)
-                send(unit, zs, far, SIB_FAR, False, exists)
-
-    for step in range(1, rows):
-        for unit in (INV, ONE, TWO):
+    def send_own(unit):
+        local[unit].wait()
+        send(unit, z, c, UP, [can_up])
+        send(unit, z, c, DOWN, [can_down])
+        send(unit, z, c, ACROSS)
+        send(unit, z, c, SIB)
+
+    def pass_along(units, step):
+        for unit in units:
             for zs, exists, lane, further in at_distance(step):
                 receive(unit, zs, c, lane, exists)
                 if step < rows - 1:
-                    send(unit, zs, c, lane, False, exists + further)
-                send(unit, zs, c, ACROSS, False, exists)
-                send(unit, zs, c, SIB, False, exists)
-        pass_across(step - 1)
-        if step == 1:
-            receive(DIAG, 0, far, ACROSS)
-            send(DIAG, 0, far, SIB_FAR)
-    pass_across(rows - 1)
-    for unit in (INV, ONE, TWO):
-        for zs in range(rows):
-            receive(unit, zs, sib, SIB)
-            receive(unit, zs, far_sib, SIB_FAR)
-    receive(DIAG, 0, sib, SIB)
-    receive(DIAG, 0, far_sib, SIB_FAR)
-    for copy in local:
+                    send(unit, zs, c, lane, exists + further)
+                send(unit, zs, c, ACROSS, exists)
+                send(unit, zs, c, SIB, exists)
+
+    def pass_across(units, step):
+        for unit in units:
+            for zs, exists, _, _ in at_distance(step):
+                receive(unit, zs, far, ACROSS, exists)
+                send(unit, zs, far, SIB_FAR, exists)
+
+    def settle(units):
+        for unit in units:
+            for zs in range(rows):
+                receive(unit, zs, sib, SIB)
+                receive(unit, zs, far_sib, SIB_FAR)
+
+    first = (INV, ONE)
+    for unit in first:
+        send_own(unit)
+    for step in range(1, rows):
+        if step == rows - 1:
+            send_own(TWO)
+        pass_along(first, step)
+        pass_across(first, step - 1)
+    for step in range(1, rows - 1):
+        pass_along((TWO,), step)
+    pass_across(first, rows - 1)
+    settle(first)
+    for copy in local[3:]:
         copy.wait()
 
     chosen = [(parent[c, 0] == k).astype(jnp.int32).astype(f32) for k in range(cols)]
@@ -365,24 +373,30 @@
 
     gather_columns(0, one_all, mask_one)
     gather_parent()
-    gather_columns(2, two_all, mask_two)
-    below = below_ref[...]
+    below = below_own[...]
 
     inner = jnp.zeros((width, width), f32)
-    inner_parent = jnp.zeros((width, width), f32)
     for r in range(rows):
         x_own = (-(mask_one(r) * times_inverse(0, r))).astype(bf16)
         x_one_all[r] = x_own
         inner += dot(masked[0, r], x_own, 0, 0)
-        x_par = (-(mask_parent(r) * times_inverse(1, r))).astype(bf16)
-        x_two_all[r] = x_par
-        inner_parent += dot(masked[1, r], x_par, 0, 0)
+    diag_one = (dinv_one[...] - inner).astype(bf16)
+    diag_all[c] = diag_one
+    send(DIAG, 0, c, ACROSS)
+    send(DIAG, 0, c, SIB)
+    pass_along((TWO,), rows - 1)
+    for r in range(rows):
+        x_two_all[r] = (-(mask_parent(r) * times_inverse(1, r))).astype(bf16)
+    for step in range(rows):
+        pass_across((TWO,), step)
+    receive(DIAG, 0, far, ACROSS)
+    send(DIAG, 0, far, SIB_FAR)
     x_one_ref[...] = x_one_all[z]
-    diag_one_ref[...] = (dinv_one_ref[...] - inner).astype(bf16)
-    dinv_parent = sum(chosen[k] * diag_all[k].astype(f32) for k in range(cols))
-    diag_parent = (dinv_parent - inner_parent).astype(bf16)
-
-    cross_part = dot(diag_parent, below)
+    diag_one_ref[...] = diag_one
+    settle((TWO,))
+    gather_columns(2, two_all, mask_two)
+
+    cross_part = jnp.zeros((width, width), f32)
     inner_two = jnp.zeros((width, width), f32)
     for r in range(rows):
         x_par = x_two_all[r]
@@ -392,9 +406,12 @@
         x_two_all[r] = x_two
         inner_two += dot(masked[2, r], x_two, 0, 0)
     x_two_ref[...] = x_two_all[z]
-    cross = (-cross_part).astype(bf16)
+    receive(DIAG, 0, sib, SIB)
+    receive(DIAG, 0, far_sib, SIB_FAR)
+    diag_parent = sum(chosen[k] * diag_all[k].astype(f32) for k in range(cols)).astype(bf16)
+    cross = (-(cross_part + dot(diag_parent, below))).astype(bf16)
     cross_ref[...] = cross
-    diag_two_ref[...] = dinv_two_ref[...] - inner_two - dot(below, cross, 0, 0)
+    diag_two_ref[...] = dinv_two[...] - inner_two - dot(below, cross, 0, 0)
 
     for conditions, descriptor in sent:
         when(conditions, lambda descriptor=descriptor: descriptor().wait_send())
@@ -418,6 +435,7 @@
     slab, wide = factor_first.shape[1:]
     square = (width, width)
     vmem = pl.BlockSpec(memory_space=pltpu.VMEM)
+    hbm = pl.BlockSpec(memory_space=pltpu.HBM)
     smem = pl.BlockSpec(memory_space=pltpu.SMEM)
     shape = jax.ShapeDtypeStruct
     return pl.pallas_call(
@@ -429,19 +447,22 @@
             shape(square, bf16),
             shape(square, jnp.float32),
         ),
-        in_specs=[vmem] * 6 + [smem] * 3,
+        in_specs=[hbm] * 6 + [smem] * 3,
         out_specs=(vmem,) * 5,
         scratch_shapes=[
             pltpu.VMEM((cols, rows * width, width), bf16),
             pltpu.VMEM((cols, rows, slab, wide), bf16),
             pltpu.VMEM((cols, rows, slab, wide), bf16),
+            pltpu.VMEM(square, bf16),
+            pltpu.VMEM(square, jnp.float32),
+            pltpu.VMEM(square, jnp.float32),
             pltpu.VMEM((cols,) + square, bf16),
             pltpu.VMEM((3, cols) + square, bf16),
             pltpu.VMEM((rows,) + square, bf16),
             pltpu.VMEM((rows,) + square, bf16),
             pltpu.SemaphoreType.DMA((4, rows, 5)),
             pltpu.SemaphoreType.DMA((4, rows, cols)),
-            pltpu.SemaphoreType.DMA((3,)),
+            pltpu.SemaphoreType.DMA((6,)),
         ],
         compiler_params=pltpu.CompilerParams(
             collective_id=0, has_side_effects=True, vmem_limit_bytes=VMEM_BUDGET

time: 54 us -> 57.3 us (1.061); the launches traced: 53 us -> 57 us
  Pallas kernels: 42.8 us -> 46.8 us
    pallas_call x1, Pallas kernels: 42.8 us -> 46.8 us  [on_device_small(): pl.pallas_call(functools.partial(fused_kernel, rows, cols), out_shape=(sh...]
where the time goes in v2:
time: 57.3 us; the launch traced here: 57 us
  Pallas kernels  46.8 us (82%)
  local copies, waits for them, and re-layouts  9.57 us (17%)
  between operations  0.67 us (1%)
    pallas_call x1, Pallas kernels, on_device_small(): pl.pallas_call(functools.partial(fused_kernel, rows, cols), out_shape=(sh...  46.8 us
    unnamed x24, local copies, waits for them, and re-layouts  9.57 us

profile of v2, /device:TPU:0, one launch (start us, length us, event | category | flops | bytes accessed | tf_op | source)
XLA Modules:
  0.0 57.0 jit_solution(2708300968485298020)
XLA Ops:
  0.6 0.0 copy-start.8
  0.6 0.0 copy-start.6
  0.7 0.0 copy-start.7
  0.7 0.6 %copy-done.8 = s32[4,1]{0,1:T(1,128)S(1)} copy-done((s32[4,1]{0,1:T(1,128)S(1)}, s32[4,1]{0,1:T(1,128)}, u32[]{:S(2)}) %copy-start.8) | copy-done | bytes 40
  1.3 0.1 copy.14.parent
  1.4 0.0 copy-done.6
  1.4 0.0 copy-done.7
  1.4 0.0 copy-start
  1.4 0.9 %copy-done = f32[256,256]{1,0:T(8,128)S(1)} copy-done((f32[256,256]{1,0:T(8,128)S(1)}, f32[256,256]{1,0:T(8,128)}, u32[]{:S(2)}) %copy-start) | copy-done | bytes 262168
  2.3 0.0 copy-start.1
  2.3 0.9 %copy-done.1 = f32[256,256]{1,0:T(8,128)S(1)} copy-done((f32[256,256]{1,0:T(8,128)S(1)}, f32[256,256]{1,0:T(8,128)}, u32[]{:S(2)}) %copy-start.1) | copy-done | bytes 262168
  3.3 0.0 copy-start.2
  3.3 0.9 %copy-done.2 = bf16[256,256]{1,0:T(8,128)(2,1)S(1)} copy-done((bf16[256,256]{1,0:T(8,128)(2,1)S(1)}, bf16[256,256]{1,0:T(8,128)(2,1)}, u32[]{:S(2)}) %copy-start.2) | copy-done | bytes 131096
  4.2 0.0 copy-start.3
  4.2 0.9 %copy-done.3 = bf16[1,64,1024]{2,1,0:T(8,128)(2,1)S(1)} copy-done((bf16[1,64,1024]{2,1,0:T(8,128)(2,1)S(1)}, bf16[1,64,1024]{2,1,0:T(8,128)(2,1)}, u32[]{:S(2)}) %copy-start.3) | copy-done | bytes 131096
  5.1 0.0 copy-start.4
  5.1 0.9 %copy-done.4 = bf16[1,64,1024]{2,1,0:T(8,128)(2,1)S(1)} copy-done((bf16[1,64,1024]{2,1,0:T(8,128)(2,1)S(1)}, bf16[1,64,1024]{2,1,0:T(8,128)(2,1)}, u32[]{:S(2)}) %copy-start.4) | copy-done | bytes 131096
  6.0 0.0 copy-start.5
  6.0 0.9 %copy-done.5 = bf16[256,256]{1,0:T(8,128)(2,1)S(1)} copy-done((bf16[256,256]{1,0:T(8,128)(2,1)S(1)}, bf16[256,256]{1,0:T(8,128)(2,1)}, u32[]{:S(2)}) %copy-start.5) | copy-done | bytes 131096
  6.9 46.8 %shard_map.128 = (bf16[256,256]{1,0:T(8,128)(2,1)S(1)}, bf16[256,256]{1,0:T(8,128)(2,1)S(1)}, bf16[256,256]{1,0:T(8,128)(2,1)S(1)}, bf16[256,256]{1,0:T(8,128)(2,1)S(1)}, f32[256,256]{1,0:T(8,128)S(1)}) custom-call(bf16[256,256]{1,0:T(8,128)(2,1)S(1)} %copy-done.2, bf16[64,1024]{1,0:T(8,128)(2,1)S(1)} %bitcast.2, bf16[64,1024]{1,0:T(8,128)(2,1)S(1)} %bitcast.3, ...), custom_call_target="tpu_custom_call" | custom-call | tf_op jit(solution)/shard_map/pallas_call | solution.py:441
  53.7 0.7 %copy.20 = bf16[256,256]{1,0:T(8,128)(2,1)} copy(bf16[256,256]{1,0:T(8,128)(2,1)S(1)} %get-tuple-element.10) | data formatting | bytes 262144
  54.4 0.7 %copy.21 = bf16[256,256]{1,0:T(8,128)(2,1)} copy(bf16[256,256]{1,0:T(8,128)(2,1)S(1)} %get-tuple-element.11) | data formatting | bytes 262144
  55.0 0.7 %copy.22 = bf16[256,256]{1,0:T(8,128)(2,1)} copy(bf16[256,256]{1,0:T(8,128)(2,1)S(1)} %get-tuple-element.12) | data formatting | bytes 262144
  55.7 0.7 %copy.23 = bf16[256,256]{1,0:T(8,128)(2,1)} copy(bf16[256,256]{1,0:T(8,128)(2,1)S(1)} %get-tuple-element.13) | data formatting | bytes 262144
  56.3 0.7 %copy.24 = f32[256,256]{1,0:T(8,128)} copy(f32[256,256]{1,0:T(8,128)S(1)} %get-tuple-element.14) | data formatting | bytes 524288
Async XLA Ops:
  0.6 0.7 %copy-start.8 = (s32[4,1]{0,1:T(1,128)S(1)}, s32[4,1]{0,1:T(1,128)}, u32[]{:S(2)}) copy-start(s32[4,1]{0,1:T(1,128)} %param.17) | copy-start | bytes 52
  0.6 0.7 %copy-start.6 = (s32[4,4]{1,0:T(4,128)S(1)}, s32[4,4]{1,0:T(4,128)}, u32[]{:S(2)}) copy-start(s32[4,4]{1,0:T(4,128)} %pat_one.1) | copy-start | bytes 196
  0.7 0.7 %copy-start.7 = (s32[4,4]{1,0:T(4,128)S(1)}, s32[4,4]{1,0:T(4,128)}, u32[]{:S(2)}) copy-start(s32[4,4]{1,0:T(4,128)} %pat_two.1) | copy-start | bytes 196
  1.4 1.0 %copy-start = (f32[256,256]{1,0:T(8,128)S(1)}, f32[256,256]{1,0:T(8,128)}, u32[]{:S(2)}) copy-start(f32[256,256]{1,0:T(8,128)} %dinv_one_ref.1) | copy-start | bytes 786436
  2.3 0.9 %copy-start.1 = (f32[256,256]{1,0:T(8,128)S(1)}, f32[256,256]{1,0:T(8,128)}, u32[]{:S(2)}) copy-start(f32[256,256]{1,0:T(8,128)} %dinv_two_ref.1) | copy-start | bytes 786436
  3.3 0.9 %copy-start.2 = (bf16[256,256]{1,0:T(8,128)(2,1)S(1)}, bf16[256,256]{1,0:T(8,128)(2,1)}, u32[]{:S(2)}) copy-start(bf16[256,256]{1,0:T(8,128)(2,1)} %inv_ref.1) | copy-start | bytes 393220
  4.2 0.9 %copy-start.3 = (bf16[1,64,1024]{2,1,0:T(8,128)(2,1)S(1)}, bf16[1,64,1024]{2,1,0:T(8,128)(2,1)}, u32[]{:S(2)}) copy-start(bf16[1,64,1024]{2,1,0:T(8,128)(2,1)} %param.10) | copy-start | bytes 393220
  5.1 0.9 %copy-start.4 = (bf16[1,64,1024]{2,1,0:T(8,128)(2,1)S(1)}, bf16[1,64,1024]{2,1,0:T(8,128)(2,1)}, u32[]{:S(2)}) copy-start(bf16[1,64,1024]{2,1,0:T(8,128)(2,1)} %param.11) | copy-start | bytes 393220
  6.0 0.9 %copy-start.5 = (bf16[256,256]{1,0:T(8,128)(2,1)S(1)}, bf16[256,256]{1,0:T(8,128)(2,1)}, u32[]{:S(2)}) copy-start(bf16[256,256]{1,0:T(8,128)(2,1)} %below_ref.1) | copy-start | bytes 393220

commit v3 on v2

--- a/solution.py
+++ b/solution.py
@@ -138,7 +138,7 @@
 
 
 MESH = pl.DeviceIdType.MESH
-VMEM_BUDGET = 48 * 1024 * 1024
+VMEM_BUDGET = 64 * 1024 * 1024
 UP, DOWN, ACROSS, SIB, SIB_FAR = range(5)
 INV, ONE, TWO, DIAG = range(4)
 
@@ -328,10 +328,10 @@
         if step == rows - 1:
             send_own(TWO)
         pass_along(first, step)
-        pass_across(first, step - 1)
     for step in range(1, rows - 1):
         pass_along((TWO,), step)
-    pass_across(first, rows - 1)
+    for step in range(rows):
+        pass_across(first, step)
     settle(first)
     for copy in local[3:]:
         copy.wait()

time: 57.3 us -> 51.2 us (0.89)
  local copies, waits for them, and re-layouts: 9.57 us -> 5.89 us
  Pallas kernels: 46.8 us -> 44.5 us
    unnamed x24 -> x16, local copies, waits for them, and re-layouts: 9.57 us -> 5.89 us
    pallas_call x1, Pallas kernels: 46.8 us -> 44.5 us  [on_device_small(): pl.pallas_call(functools.partial(fused_kernel, rows, cols), out_shape=(sh...]
where the time goes in v3:
time: 51.2 us; the launch traced here: 51 us
  Pallas kernels  44.5 us (87%)
  local copies, waits for them, and re-layouts  5.89 us (12%)
  between operations  0.66 us (1%)
    pallas_call x1, Pallas kernels, on_device_small(): pl.pallas_call(functools.partial(fused_kernel, rows, cols), out_shape=(sh...  44.5 us
    unnamed x16, local copies, waits for them, and re-layouts  5.89 us

profile of v3, /device:TPU:0, one launch (start us, length us, event | category | flops | bytes accessed | tf_op | source)
XLA Modules:
  0.0 51.0 jit_solution(525887155973460444)
XLA Ops:
  0.6 0.0 copy-start.4
  0.6 0.6 %copy-done.4 = s32[4,1]{0,1:T(1,128)S(1)} copy-done((s32[4,1]{0,1:T(1,128)S(1)}, s32[4,1]{0,1:T(1,128)}, u32[]{:S(2)}) %copy-start.4) | copy-done | bytes 40
  1.3 0.7 %copy.14.parent = s32[4,1]{1,0:T(4,128)} copy(s32[4,1]{0,1:T(1,128)S(1)} %copy-done.4) | data formatting | bytes 32 | tf_op args[8]
  2.0 44.5 %shard_map.128 = (bf16[256,256]{1,0:T(8,128)(2,1)}, bf16[256,256]{1,0:T(8,128)(2,1)}, bf16[256,256]{1,0:T(8,128)(2,1)}, bf16[256,256]{1,0:T(8,128)(2,1)}, f32[256,256]{1,0:T(8,128)}) custom-call(bf16[256,256]{1,0:T(8,128)(2,1)} %inv_ref.1, bf16[64,1024]{1,0:T(8,128)(2,1)} %bitcast.2, bf16[64,1024]{1,0:T(8,128)(2,1)} %bitcast.3, bf16[256,256]{1,0:T(8,128)(2,1)} %below_ref.1, ...), custom_call_target="tpu_custom_call" | custom-call | tf_op jit(solution)/shard_map/pallas_call | solution.py:441
  46.5 0.0 copy-start.3
  46.5 1.6 %copy.20 = bf16[256,256]{1,0:T(8,128)(2,1)} copy(bf16[256,256]{1,0:T(8,128)(2,1)} %get-tuple-element.10) | data formatting | bytes 262144
  48.1 0.0 copy-done.3
  48.1 0.0 copy-start.2
  48.1 0.0 copy-start.1
  48.1 0.7 %copy.21 = bf16[256,256]{1,0:T(8,128)(2,1)} copy(bf16[256,256]{1,0:T(8,128)(2,1)S(1)} %copy-done.3) | data formatting | bytes 262144
  48.7 0.3 copy-done.2
  49.0 0.0 copy-start
  49.0 0.7 %copy.22 = bf16[256,256]{1,0:T(8,128)(2,1)} copy(bf16[256,256]{1,0:T(8,128)(2,1)S(1)} %copy-done.2) | data formatting | bytes 262144
  49.7 0.0 copy-done.1
  49.7 0.7 %copy.23 = bf16[256,256]{1,0:T(8,128)(2,1)} copy(bf16[256,256]{1,0:T(8,128)(2,1)S(1)} %copy-done.1) | data formatting | bytes 262144
  50.3 0.0 copy-done
  50.3 0.7 %copy.24 = f32[256,256]{1,0:T(8,128)} copy(f32[256,256]{1,0:T(8,128)S(1)} %copy-done) | data formatting | bytes 524288
Async XLA Ops:
  0.6 0.7 %copy-start.4 = (s32[4,1]{0,1:T(1,128)S(1)}, s32[4,1]{0,1:T(1,128)}, u32[]{:S(2)}) copy-start(s32[4,1]{0,1:T(1,128)} %param.17) | copy-start | bytes 52
  46.5 1.6 %copy-start.3 = (bf16[256,256]{1,0:T(8,128)(2,1)S(1)}, bf16[256,256]{1,0:T(8,128)(2,1)}, u32[]{:S(2)}) copy-start(bf16[256,256]{1,0:T(8,128)(2,1)} %get-tuple-element.11) | copy-start | bytes 393220
  48.1 1.0 %copy-start.2 = (bf16[256,256]{1,0:T(8,128)(2,1)S(1)}, bf16[256,256]{1,0:T(8,128)(2,1)}, u32[]{:S(2)}) copy-start(bf16[256,256]{1,0:T(8,128)(2,1)} %get-tuple-element.12) | copy-start | bytes 393220
  48.1 1.6 %copy-start.1 = (bf16[256,256]{1,0:T(8,128)(2,1)S(1)}, bf16[256,256]{1,0:T(8,128)(2,1)}, u32[]{:S(2)}) copy-start(bf16[256,256]{1,0:T(8,128)(2,1)} %get-tuple-element.13) | copy-start | bytes 393220
  49.0 1.3 %copy-start = (f32[256,256]{1,0:T(8,128)S(1)}, f32[256,256]{1,0:T(8,128)}, u32[]{:S(2)}) copy-start(f32[256,256]{1,0:T(8,128)} %get-tuple-element.14) | copy-start | bytes 786436

commit v4 on v3

--- a/solution.py
+++ b/solution.py
@@ -417,6 +417,12 @@
         when(conditions, lambda descriptor=descriptor: descriptor().wait_send())
 
 
+def place_results(*refs):
+    count = len(refs) // 2
+    for slot in range(count):
+        refs[count + slot][...] = refs[slot][...]
+
+
 def on_device_small(
     rows,
     cols,
@@ -438,7 +444,7 @@
     hbm = pl.BlockSpec(memory_space=pltpu.HBM)
     smem = pl.BlockSpec(memory_space=pltpu.SMEM)
     shape = jax.ShapeDtypeStruct
-    return pl.pallas_call(
+    results = pl.pallas_call(
         functools.partial(fused_kernel, rows, cols),
         out_shape=(
             shape(square, bf16),
@@ -478,6 +484,12 @@
         pattern_second,
         parent,
     )
+    return pl.pallas_call(
+        place_results,
+        out_shape=tuple(shape(result.shape, result.dtype) for result in results),
+        in_specs=[vmem] * 5,
+        out_specs=(vmem,) * 5,
+    )(*results)
 
 
 def on_device(rows, cols, *args):

time: 51.2 us -> 48.7 us (0.951)
  local copies, waits for them, and re-layouts: 5.89 us -> 1.31 us
  Pallas kernels: 44.5 us -> 46.6 us
    unnamed x16 -> x3, local copies, waits for them, and re-layouts: 5.89 us -> 1.31 us
    pallas_call x0 -> x1, Pallas kernels: none -> 2.1 us  [on_device_small(): pl.pallas_call(place_results, out_shape=tuple((shape(result.shape, result...]
where the time goes in v4:
time: 48.7 us; the launch traced here: 48.5 us
  Pallas kernels  46.6 us (96%)
  local copies, waits for them, and re-layouts  1.31 us (3%)
  between operations  0.65 us (1%)
    pallas_call x1, Pallas kernels, on_device_small(): pl.pallas_call(functools.partial(fused_kernel, rows, cols), out_shape=(sh...  44.5 us
    pallas_call x1, Pallas kernels, on_device_small(): pl.pallas_call(place_results, out_shape=tuple((shape(result.shape, result...  2.1 us
    unnamed x3, local copies, waits for them, and re-layouts  1.31 us

profile of v4, /device:TPU:0, one launch (start us, length us, event | category | flops | bytes accessed | tf_op | source)
XLA Modules:
  0.0 48.5 jit_solution(2641796294299591738)
XLA Ops:
  0.6 0.0 copy-start
  0.6 0.6 %copy-done = s32[4,1]{0,1:T(1,128)S(1)} copy-done((s32[4,1]{0,1:T(1,128)S(1)}, s32[4,1]{0,1:T(1,128)}, u32[]{:S(2)}) %copy-start) | copy-done | bytes 40
  1.3 0.7 %copy.14.parent = s32[4,1]{1,0:T(4,128)} copy(s32[4,1]{0,1:T(1,128)S(1)} %copy-done) | data formatting | bytes 32 | tf_op args[8]
  2.0 44.5 %shard_map.128 = (bf16[256,256]{1,0:T(8,128)(2,1)}, bf16[256,256]{1,0:T(8,128)(2,1)}, bf16[256,256]{1,0:T(8,128)(2,1)}, bf16[256,256]{1,0:T(8,128)(2,1)}, f32[256,256]{1,0:T(8,128)}) custom-call(bf16[256,256]{1,0:T(8,128)(2,1)} %inv_ref.1, bf16[64,1024]{1,0:T(8,128)(2,1)} %bitcast.2, bf16[64,1024]{1,0:T(8,128)(2,1)} %bitcast.3, bf16[256,256]{1,0:T(8,128)(2,1)} %below_ref.1, ...), custom_call_target="tpu_custom_call" | custom-call | tf_op jit(solution)/shard_map/pallas_call | solution.py:447
  46.4 2.1 %shard_map.129 = (bf16[256,256]{1,0:T(8,128)(2,1)}, bf16[256,256]{1,0:T(8,128)(2,1)}, bf16[256,256]{1,0:T(8,128)(2,1)}, bf16[256,256]{1,0:T(8,128)(2,1)}, f32[256,256]{1,0:T(8,128)}) custom-call(bf16[256,256]{1,0:T(8,128)(2,1)} %get-tuple-element.10.refs_0_, bf16[256,256]{1,0:T(8,128)(2,1)} %get-tuple-element.11.refs_1_, ...), custom_call_target="tpu_custom_call" | custom-call | tf_op jit(solution)/shard_map/pallas_call | solution.py:487
Async XLA Ops:
  0.6 0.7 %copy-start = (s32[4,1]{0,1:T(1,128)S(1)}, s32[4,1]{0,1:T(1,128)}, u32[]{:S(2)}) copy-start(s32[4,1]{0,1:T(1,128)} %param.17) | copy-start | bytes 52

commit v5 on v4

--- a/solution.py
+++ b/solution.py
@@ -385,15 +385,16 @@
     send(DIAG, 0, c, ACROSS)
     send(DIAG, 0, c, SIB)
     pass_along((TWO,), rows - 1)
+    for step in range(rows - 1):
+        pass_across((TWO,), step)
     for r in range(rows):
         x_two_all[r] = (-(mask_parent(r) * times_inverse(1, r))).astype(bf16)
-    for step in range(rows):
-        pass_across((TWO,), step)
-    receive(DIAG, 0, far, ACROSS)
-    send(DIAG, 0, far, SIB_FAR)
+    pass_across((TWO,), rows - 1)
     x_one_ref[...] = x_one_all[z]
     diag_one_ref[...] = diag_one
     settle((TWO,))
+    receive(DIAG, 0, far, ACROSS)
+    send(DIAG, 0, far, SIB_FAR)
     gather_columns(2, two_all, mask_two)
 
     cross_part = jnp.zeros((width, width), f32)

time: 48.7 us -> 48.7 us (level)
  no operation moved by 1% of the time
where the time goes in v5:
time: 48.7 us; the launch traced here: 48.5 us
  Pallas kernels  46.6 us (96%)
  local copies, waits for them, and re-layouts  1.31 us (3%)
  between operations  0.65 us (1%)
    pallas_call x1, Pallas kernels, on_device_small(): pl.pallas_call(functools.partial(fused_kernel, rows, cols), out_shape=(sh...  44.5 us
    pallas_call x1, Pallas kernels, on_device_small(): pl.pallas_call(place_results, out_shape=tuple((shape(result.shape, result...  2.1 us
    unnamed x3, local copies, waits for them, and re-layouts  1.31 us

profile of v5, /device:TPU:0, one launch (start us, length us, event | category | flops | bytes accessed | tf_op | source)
XLA Modules:
  0.0 48.5 jit_solution(8379631746143510708)
XLA Ops:
  0.6 0.0 copy-start
  0.6 0.6 %copy-done = s32[4,1]{0,1:T(1,128)S(1)} copy-done((s32[4,1]{0,1:T(1,128)S(1)}, s32[4,1]{0,1:T(1,128)}, u32[]{:S(2)}) %copy-start) | copy-done | bytes 40
  1.3 0.7 %copy.14.parent = s32[4,1]{1,0:T(4,128)} copy(s32[4,1]{0,1:T(1,128)S(1)} %copy-done) | data formatting | bytes 32 | tf_op args[8]
  2.0 44.5 %shard_map.128 = (bf16[256,256]{1,0:T(8,128)(2,1)}, bf16[256,256]{1,0:T(8,128)(2,1)}, bf16[256,256]{1,0:T(8,128)(2,1)}, bf16[256,256]{1,0:T(8,128)(2,1)}, f32[256,256]{1,0:T(8,128)}) custom-call(bf16[256,256]{1,0:T(8,128)(2,1)} %inv_ref.1, bf16[64,1024]{1,0:T(8,128)(2,1)} %bitcast.2, bf16[64,1024]{1,0:T(8,128)(2,1)} %bitcast.3, bf16[256,256]{1,0:T(8,128)(2,1)} %below_ref.1, ...), custom_call_target="tpu_custom_call" | custom-call | tf_op jit(solution)/shard_map/pallas_call | solution.py:448
  46.4 2.1 %shard_map.129 = (bf16[256,256]{1,0:T(8,128)(2,1)}, bf16[256,256]{1,0:T(8,128)(2,1)}, bf16[256,256]{1,0:T(8,128)(2,1)}, bf16[256,256]{1,0:T(8,128)(2,1)}, f32[256,256]{1,0:T(8,128)}) custom-call(bf16[256,256]{1,0:T(8,128)(2,1)} %get-tuple-element.10.refs_0_, bf16[256,256]{1,0:T(8,128)(2,1)} %get-tuple-element.11.refs_1_, ...), custom_call_target="tpu_custom_call" | custom-call | tf_op jit(solution)/shard_map/pallas_call | solution.py:488
Async XLA Ops:
  0.6 0.7 %copy-start = (s32[4,1]{0,1:T(1,128)S(1)}, s32[4,1]{0,1:T(1,128)}, u32[]{:S(2)}) copy-start(s32[4,1]{0,1:T(1,128)} %param.17) | copy-start | bytes 52
